TPU v7x, 32 devices: a whole 2x2x4 slice. The times are simulated.
32 devices in a mesh: tile: 16 (over z, y, core), freq: 2 (over x).
Axes of the slice: x: 2, y: 2, z: 4, core: 2. Of those that a mesh axis runs over, the one named last changes fastest.
Arguments:
- visibilities: float32 [2, 2048, 2, 128], P('freq', 'tile'), may hold values from -6 to 6
- uv_cell: int32 [2, 2048, 2, 128], P('freq', 'tile'), may hold values from 0 to 120
- sub_pixel: int32 [2, 2048, 2, 128], P('freq', 'tile'), may hold values from 0 to 7
- w_plane: int32 [2, 2048], P('freq', 'tile'), may hold values from 0 to 15
- block_tile: int32 [2, 2048], P('freq', 'tile'), may hold values from 0 to 31, as said below
- model_grid: bfloat16 [2, 32, 128, 256], P('freq', 'tile'), may hold values from -3 to 3
- kernel_table: bfloat16 [16, 8, 8], replicated, may hold values from 0.049804688 to 1
- coupling: float32 [2, 2], replicated, may hold values from -4 to 4
Outputs:
- residuals: float32 [2, 2048, 2, 128], P('freq', 'tile')
- coupled_grid: float32 [2, 32, 128, 256], P('freq', 'tile')
Inputs may be any that keep to these rules, and one draw needn't show every extreme that they name: `block_tile`: among the 128 blocks of one plane on one device (aligned blocks), at most 24 have tiles of one owner, the owner of tile k being k // 2; in every plane some owner gets exactly 24 blocks from every device.
All inputs are finite; a program needn't handle non-finite values.
Results may differ from a plain program's by a relative error of at most 0.0034.
Values may be sent and summed in bfloat16 or wider, within the bound.
No kernel may reach another device: no remote copies, remote signals or barrier semaphores. Data moves between devices by JAX's collectives and lax.ppermute only.
A program may use at most 64 MiB of HBM per device.

v0:
```python
import jax
import jax.numpy as jnp
from jax import lax
from jax.experimental import pallas as pl
from jax.experimental.pallas import tpu as pltpu
from jax.sharding import PartitionSpec as P

UNROLL = 2
CHUNKS = 35
AHEAD = 2
BUFFERS = 5
VMEM = pl.BlockSpec(memory_space=pltpu.VMEM)
SMEM = pl.BlockSpec(memory_space=pltpu.SMEM)
HBM = pl.BlockSpec(memory_space=pltpu.HBM)
PARAMS = pltpu.CompilerParams(vmem_limit_bytes=32 * 1024 * 1024)
WHOLE_PARAMS = pltpu.CompilerParams(vmem_limit_bytes=62 * 1024 * 1024)
TILE_SHIFT = 12
PLANE_SHIFT = 16
SOURCE_SHIFT = 21
FULL = 32767
SCALE = 2.0**20


def scalar_div(value, count):
    shift = count.bit_length() - 1
    return value >> shift if count == 1 << shift else lax.div(value, count)


def first_slot(local, rank, capacity):
    half = capacity // 2
    return (local >> 1) * half + jnp.where((local & 1) == 0, rank, half - 1 - rank)


def rows_per_source(capacity):
    return (3 * (capacity + 1) + 7) // 8 * 8


def two_halves(high, low):
    return (high << 16) | (low & 0xFFFF)


def pack_kernel(pairs, capacity, tiles_here, plane_hbm, tile_hbm, vis_hbm, cell_hbm, sub_hbm,
                sent_ref, slot_ref, row_ref, plane_ref, tile_ref, vis_ref, cell_ref, sub_ref, code_ref,
                count_ref, load_sem):
    blocks = tile_ref.shape[0]
    stride = rows_per_source(capacity)
    tiles = 2 * tiles_here
    lane = lax.broadcasted_iota(jnp.int32, (1, 128), 1)
    loads = [
        pltpu.make_async_copy(source, target, load_sem.at[i])
        for i, (source, target) in enumerate(
            [
                (tile_hbm, tile_ref),
                (plane_hbm, plane_ref),
                (vis_hbm, vis_ref),
                (cell_hbm, cell_ref),
                (sub_hbm, sub_ref),
            ]
        )
    ]
    for copy in loads:
        copy.start()
    for key in range(pairs * tiles):
        count_ref[key] = 0
    for copy in loads:
        copy.wait()

    def assign(b):
        tile = tile_ref[b]
        owner = scalar_div(tile, tiles_here)
        high = (owner >= pairs).astype(jnp.int32)
        pair = owner - high * pairs
        local = tile - (owner - high) * tiles_here
        key = pair * tiles + local
        rank = count_ref[key]
        count_ref[key] = rank + 1
        place = first_slot(local, rank, capacity)
        slot_ref[b] = pair * (capacity + 1) + place
        row_ref[b] = pair * stride + 3 * place
        codes = code_ref[pl.ds(pair, 1), :]
        code_ref[pl.ds(pair, 1), :] = jnp.where(lane == place, plane_ref[b] << PLANE_SHIFT, codes)

    largest = jnp.max(jnp.max(jnp.abs(vis_ref[...]), axis=0, keepdims=True), axis=1, keepdims=True)
    largest = jnp.maximum(jnp.ceil(largest * SCALE), 1.0)
    inverse = (FULL * SCALE) / largest

    def move(four):
        rows = pl.ds(pl.multiple_of(8 * four, 8), 8)
        value = jnp.clip(jnp.round(vis_ref[rows, :] * inverse), -FULL, FULL).astype(jnp.int32)
        words = [
            two_halves(parts, pltpu.roll(parts, 7, 0))
            for parts in [value, cell_ref[rows, :], sub_ref[rows, :]]
        ]
        for u in range(4):
            row = row_ref[4 * four + u]
            for i, word in enumerate(words):
                sent_ref[pl.ds(row + i, 1), :] = word[2 * u : 2 * u + 1]

    def step(turn, carry):
        for which in range(8):
            assign(8 * turn + 8 + which)
        move(2 * turn)
        move(2 * turn + 1)
        return carry

    for which in range(8):
        assign(which)
    lax.fori_loop(0, blocks // 8 - 1, step, 0)
    move(blocks // 4 - 2)
    move(blocks // 4 - 1)
    for d in range(pairs):
        counts = jnp.broadcast_to(largest.astype(jnp.int32), (1, 128))
        for t in range(tiles):
            counts = jnp.where(lane == t, count_ref[d * tiles + t], counts)
        row = d * stride + 3 * capacity
        sent_ref[row : row + 1, :] = code_ref[d : d + 1, :]
        sent_ref[row + 1 : row + 2, :] = jnp.zeros((1, 128), jnp.int32)
        sent_ref[row + 2 : row + 3, :] = counts


def finish_kernel(row_ref, slot_ref, returned_ref, grid_ref, residual_ref, coupled_ref):
    planes, tiles_here = grid_ref.shape[:2]
    for t in range(tiles_here):
        coupled_ref[t] = sum(
            row_ref[g] * grid_ref[g, t].astype(jnp.float32) for g in range(planes)
        ).T

    def step(turn, carry):
        for which in range(8):
            b = turn * 8 + which
            residual_ref[b] = returned_ref[slot_ref[b]].astype(jnp.float32)
        return carry

    lax.fori_loop(0, residual_ref.shape[0] // 8, step, 0)


def spread_parts(start, offset, table):
    sublane = lax.broadcasted_iota(jnp.int32, (8, 128), 0)
    taps, group = [], []
    for low in (0, 8):
        delta = sublane + low - start
        taps.append(
            jnp.take_along_axis(table, (delta & 15) + offset, axis=1, mode="promise_in_bounds")
        )
        group.append((15 - delta) >> 4)
    return jnp.concatenate(taps, axis=0), jnp.concatenate(group, axis=0)


def grid_kernel(pairs, capacity, member_ref, got_ref, table_ref, model_ref, residual_ref, own_ref,
                other_ref, turned_ref, grid_ref, code_ref, about_ref, list_ref, sem, *buffers):
    row_refs, picked_refs = buffers[:BUFFERS], buffers[BUFFERS:]
    tiles, side, wide = model_ref.shape
    groups = side // 16
    zero_row = table_ref.shape[0] - 8
    stride = rows_per_source(capacity)
    lane = lax.broadcasted_iota(jnp.int32, (1, 128), 1)
    for s in range(pairs):
        row = s * stride + 3 * capacity
        code_ref[s, 0:1, :] = got_ref[row : row + 1, :] + (
            lane + s * (capacity + 1) + (s << SOURCE_SHIFT)
        )
        code_ref[s, 1:2, :] = got_ref[row + 2 : row + 3, :]
    fill = pltpu.make_async_copy(code_ref, about_ref, sem)
    fill.start()
    for t in range(tiles):
        turned_ref[t] = model_ref[t].T
    grid_ref[...] = jnp.zeros_like(grid_ref)
    fill.wait()

    start = jnp.int32(0)
    for t in range(tiles):
        count = jnp.int32(0)
        for s in range(pairs):
            count = count + about_ref[s, 1, t]
        spare = -count & (UNROLL - 1)
        for u in range(UNROLL):
            list_ref[start + u] = (zero_row << PLANE_SHIFT) + (t << TILE_SHIFT) + capacity

        def enlist(s, filled, t=t):
            found = about_ref[s, 1, t]

            def some(low, high):
                for k in range(low, high):
                    place = k if t % 2 == 0 else capacity // 2 - 1 - k
                    code = about_ref[s, 0, t // 2 * (capacity // 2) + place]
                    list_ref[filled + k] = code + (t << TILE_SHIFT)

            few = capacity // 3

            @pl.when(found > 0)
            def _():
                some(0, few)

                @pl.when(found > few)
                def _():
                    some(few, capacity // 2)

            return filled + found

        lax.fori_loop(0, pairs, enlist, start + spare)
        start = start + count + spare
    for u in range((CHUNKS + AHEAD) * UNROLL):
        list_ref[start + u] = (zero_row << PLANE_SHIFT) + capacity
    chunks = start >> UNROLL.bit_length() - 1
    zero = jnp.zeros((16, 128), jnp.bfloat16)

    def read(which):
        entry = list_ref[which]
        slot = entry & ((1 << TILE_SHIFT) - 1)
        plane = (entry >> PLANE_SHIFT) & ((1 << (SOURCE_SHIFT - PLANE_SHIFT)) - 1)
        source = entry >> SOURCE_SHIFT
        row = 3 * slot + source * (stride - 3 * (capacity + 1))
        table = jnp.broadcast_to(table_ref[pl.ds(plane, 1), :], (8, 128))

        def words(i):
            return got_ref[pl.ds(row + i, 1), :]

        def parts(shift):
            start = (words(1) >> shift) & 0xFFFF
            offset = ((words(2) >> shift) & 7) << 4
            return spread_parts(
                jnp.broadcast_to(start, (8, 128)), jnp.broadcast_to(offset, (8, 128)), table
            )

        def sample(part):
            step = about_ref[source, 1, tiles].astype(jnp.float32) * (1.0 / (FULL * SCALE))
            return ((words(0) << (16 * part)) >> 16).astype(jnp.float32) * step

        return slot, sample, parts

    def chunk_tile(turn):
        return (list_ref[turn * UNROLL] >> TILE_SHIFT) & 15

    def front(turn, which):
        row_ref, picked_ref = row_refs[which % len(row_refs)], picked_refs[which % len(picked_refs)]
        blocks = [read(turn * UNROLL + u) for u in range(UNROLL)]
        matrices = []
        for _, _, parts in blocks:
            taps, group = parts(16)
            taps = taps.astype(jnp.bfloat16)
            group = group.astype(jnp.float32).astype(jnp.bfloat16)
            matrices.append(
                jnp.concatenate([jnp.where(group == k, taps, zero) for k in range(groups)], axis=0)
            )
        row_matrix = jnp.concatenate(matrices, axis=1)
        row_ref[...] = row_matrix
        partial = jnp.dot(
            turned_ref[chunk_tile(turn)], row_matrix, preferred_element_type=jnp.float32
        )
        for u, (_, _, parts) in enumerate(blocks):
            columns = slice(128 * u, 128 * u + 128)
            taps, group = parts(0)
            for part in range(2):
                picked = jnp.zeros((16, 128), jnp.float32)
                for k in range(groups):
                    low = part * side + 16 * k
                    picked = jnp.where(group == k, partial[low : low + 16, columns], picked)
                picked_ref[part, :, columns] = picked * taps

    def back(turn, which):
        row_ref, picked_ref = row_refs[which % len(row_refs)], picked_refs[which % len(picked_refs)]
        weighted = []
        for u in range(UNROLL):
            slot, sample, parts = read(turn * UNROLL + u)
            columns = slice(128 * u, 128 * u + 128)
            taps, group = parts(0)
            group = group.astype(jnp.float32).astype(jnp.bfloat16)
            residuals, pieces = [], []
            for part in range(2):
                model = jnp.sum(picked_ref[part, :, columns], axis=0, keepdims=True)
                residual = sample(part) - model
                residuals.append(residual)
                value = (residual * taps).astype(jnp.bfloat16)
                pieces += [jnp.where(group == k, value, zero) for k in range(groups)]
            residual_ref[slot] = jnp.concatenate(residuals, axis=0).astype(jnp.bfloat16)
            weighted.append(jnp.concatenate(pieces, axis=0))
        grid_ref[chunk_tile(turn)] += lax.dot_general(
            jnp.concatenate(weighted, axis=1),
            row_ref[...],
            (((1,), (1,)), ((), ())),
            preferred_element_type=jnp.float32,
        )

    def step(turn, carry):
        for which in range(CHUNKS):
            front(turn * CHUNKS + which + AHEAD, which + AHEAD)
            back(turn * CHUNKS + which, which)
        return carry

    for which in range(AHEAD):
        front(which, which)
    lax.fori_loop(0, scalar_div(chunks + CHUNKS - 1, CHUNKS), step, 0)
    half = tiles // 2
    member = member_ref[0]
    for t in range(half):
        own_ref[t] = grid_ref[member * half + t]
        other_ref[t] = grid_ref[(1 - member) * half + t].astype(jnp.bfloat16)


def body(visibilities, uv_cell, sub_pixel, w_plane, block_tile, model_grid, kernel_table, coupling):
    owners = lax.axis_size("tile")
    pairs = owners // 2
    _, blocks, _, rows = visibilities.shape
    capacity = 2 * (3 * blocks // owners)
    _, tiles_here, side, wide = model_grid.shape
    planes, oversample, support = kernel_table.shape
    slots = pairs * (capacity + 1)
    member = lax.axis_index("tile") // pairs
    swap = [(t, (t + pairs) % owners) for t in range(owners)]
    halves = [list(range(pairs)), list(range(pairs, owners))]

    model = lax.all_gather(
        model_grid[0],
        "tile",
        axis=0,
        tiled=True,
        axis_index_groups=[[t, t + pairs] for t in range(pairs)],
    )
    sent, slot = pl.pallas_call(
        lambda *refs: pack_kernel(pairs, capacity, tiles_here, *refs),
        out_shape=(
            jax.ShapeDtypeStruct((pairs * rows_per_source(capacity), rows), jnp.int32),
            jax.ShapeDtypeStruct((blocks,), jnp.int32),
        ),
        in_specs=[HBM] * 5,
        out_specs=(VMEM, SMEM),
        scratch_shapes=[
            pltpu.SMEM((blocks,), jnp.int32),
            pltpu.SMEM((blocks,), jnp.int32),
            pltpu.SMEM((blocks,), jnp.int32),
            pltpu.VMEM((2 * blocks, rows), jnp.float32),
            pltpu.VMEM((2 * blocks, rows), jnp.int32),
            pltpu.VMEM((2 * blocks, rows), jnp.int32),
            pltpu.VMEM((pairs, rows), jnp.int32),
            pltpu.SMEM((pairs * 2 * tiles_here,), jnp.int32),
            pltpu.SemaphoreType.DMA((5,)),
        ],
        compiler_params=WHOLE_PARAMS,
        name="pack_blocks",
    )(
        w_plane[0],
        block_tile[0],
        *[array.reshape(2 * blocks, rows) for array in (visibilities, uv_cell, sub_pixel)],
    )
    got = lax.all_to_all(
        sent, "tile", split_axis=0, concat_axis=0, tiled=True, axis_index_groups=halves
    )
    own_row = lax.dynamic_index_in_dim(coupling, lax.axis_index("freq"), 0, keepdims=False)
    slot, own_row, got = lax.optimization_barrier(
        (slot + lax.div(lax.axis_index("tile"), owners), own_row, got)
    )
    table = jnp.pad(
        kernel_table.astype(jnp.float32), ((0, 8), (0, 0), (0, 16 - support))
    ).reshape(planes + 8, 16 * oversample)
    residual, own, other = pl.pallas_call(
        lambda *refs: grid_kernel(pairs, capacity, *refs),
        out_shape=(
            jax.ShapeDtypeStruct((slots, 2, rows), jnp.bfloat16),
            jax.ShapeDtypeStruct((tiles_here, wide, side), jnp.float32),
            jax.ShapeDtypeStruct((tiles_here, wide, side), jnp.bfloat16),
        ),
        in_specs=[SMEM, VMEM, VMEM, VMEM],
        out_specs=(VMEM, VMEM, VMEM),
        scratch_shapes=[
            pltpu.VMEM((2 * tiles_here, wide, side), jnp.bfloat16),
            pltpu.VMEM((2 * tiles_here, wide, side), jnp.float32),
            pltpu.VMEM((pairs, 2, rows), jnp.int32),
            pltpu.SMEM((pairs, 2, rows), jnp.int32),
            pltpu.SMEM(
                (slots + capacity + (2 * tiles_here + CHUNKS + AHEAD) * UNROLL,), jnp.int32
            ),
            pltpu.SemaphoreType.DMA,
            *[pltpu.VMEM((side, UNROLL * rows), jnp.bfloat16)] * BUFFERS,
            *[pltpu.VMEM((2, 16, UNROLL * rows), jnp.float32)] * BUFFERS,
        ],
        compiler_params=PARAMS,
        name="grid_blocks",
    )(member[None], got, table, model)

    returned = lax.all_to_all(
        residual, "tile", split_axis=0, concat_axis=0, tiled=True, axis_index_groups=halves
    )
    grid_sum = own + lax.ppermute(other, "tile", swap).astype(jnp.float32)
    grids = lax.all_gather(grid_sum.astype(jnp.bfloat16)[None], "freq", axis=0, tiled=True)
    residuals, coupled_grid = pl.pallas_call(
        finish_kernel,
        out_shape=(
            jax.ShapeDtypeStruct((blocks, 2, rows), jnp.float32),
            jax.ShapeDtypeStruct((tiles_here, side, wide), jnp.float32),
        ),
        in_specs=[SMEM, SMEM, VMEM, VMEM],
        out_specs=(VMEM, VMEM),
        compiler_params=PARAMS,
        name="finish",
    )(own_row, slot, returned, grids)
    return (residuals[None], coupled_grid[None])


def solution(mesh):
    return jax.shard_map(
        body,
        mesh=mesh,
        in_specs=(
            P("freq", "tile", None, None),
            P("freq", "tile", None, None),
            P("freq", "tile", None, None),
            P("freq", "tile"),
            P("freq", "tile"),
            P("freq", "tile", None, None),
            P(),
            P(),
        ),
        out_specs=(P("freq", "tile", None, None), P("freq", "tile", None, None)),
        check_vma=False,
    )
```

profile of v0, /device:TPU:0, one launch (start us, length us, event | category | flops | bytes accessed | tf_op | source)
XLA Modules:
  0.0 49.6 jit_solution(4657600482829161078)
XLA Ops:
  0.6 0.0 copy-start
  0.6 3.4 %pack_blocks.1 = (s32[1216,128]{1,0:T(8,128)}, s32[128]{0:T(128)}) custom-call(s32[128]{0:T(128)} %bitcast.26, s32[128]{0:T(128)} %bitcast.27, f32[256,128]{1,0:T(8,128)} %bitcast.22, s32[256,128]{1,0:T(8,128)} %bitcast.23, s32[256,128]{1,0:T(8,128)} %bitcast.24), custom_call_target="tpu_custom_call" | custom-call | tf_op jit(solution)/shard_map/pack_blocks/pallas_call | solution.py:319
  4.0 5.3 %all-to-all-start = ((s32[8,152,128]{2,1,0:T(8,128)}), s32[8,152,128]{2,1,0:T(8,128)S(1)}, u32[]{:S(2)}, u32[]{:S(2)}) async-start(s32[8,152,128]{2,1,0:T(8,128)} %bitcast.21), calls=%async_computation | async-start | bytes 1245184 | tf_op jit(solution)/shard_map/all_to_all | solution.py:345
  9.3 0.0 copy-start.2
  9.3 0.0 copy-start.1
  9.3 0.7 %copy-done.2 = bf16[16,8,8]{0,2,1:T(8,128)(2,1)S(1)} copy-done((bf16[16,8,8]{0,2,1:T(8,128)(2,1)S(1)}, bf16[16,8,8]{0,2,1:T(8,128)(2,1)}, u32[]{:S(2)}) %copy-start.2) | copy-done | bytes 2072
  10.1 0.1 copy.14.refs_2_
  10.1 0.1 copy-done.1
  10.2 9.7 %all-gather = bf16[1,4,128,256]{3,2,0,1:T(8,128)(2,1)S(1)} all-gather(bf16[1,2,128,256]{3,2,0,1:T(8,128)(2,1)S(1)} %bitcast.25), channel_id=2, replica_groups={{0,16},{2,18},{4,20},{6,22},{8,24},{10,26},{12,28},{14,30},{1,17},{3,19..., dimensions={1}, use_global_device_ids=true | all-gather | bytes 393216 | tf_op jit(solution)/shard_map/all_gather | solution.py:312
  19.9 0.0 copy-done
  20.0 0.0 copy-start.3
  20.0 0.6 %copy-done.3 = s32[128]{0:T(128)S(1)} copy-done((s32[128]{0:T(128)S(1)}, s32[128]{0:T(128)}, u32[]{:S(2)}) %copy-start.3) | copy-done | bytes 536
  20.6 1.4 %all-to-all-done = s32[8,152,128]{2,1,0:T(8,128)S(1)} async-done(((s32[8,152,128]{2,1,0:T(8,128)}), s32[8,152,128]{2,1,0:T(8,128)S(1)}, u32[]{:S(2)}, u32[]{:S(2)}) %all-to-all-start) | async-done | bytes 622624 | tf_op jit(solution)/shard_map/all_to_all | solution.py:345
  22.0 11.5 %grid_blocks.1 = (bf16[392,2,128]{2,1,0:T(2,128)(2,1)}, f32[2,256,128]{2,1,0:T(8,128)S(1)}, bf16[2,256,128]{2,1,0:T(8,128)(2,1)S(1)}) custom-call(s32[1]{0:T(128)} %bitcast.8.refs_0_, s32[1216,128]{1,0:T(8,128)S(1)} %bitcast.18, f32[24,128]{1,0:T(8,128)S(1)} %copy.14.refs_2_, bf16[4,128,256]{2,1,0:T(8,128)(2,1)S(1)} %bitcast.19), custom_call_target="tpu_custom_call" | custom-call | tf_op jit(solution)/shard_map/grid_blocks/pallas_call | solution.py:355
  33.5 2.1 %collective-permute-start = (bf16[2,256,128]{2,1,0:T(8,128)(2,1)S(1)}, bf16[2,256,128]{2,1,0:T(8,128)(2,1)S(1)}, u32[]{:S(2)}, u32[]{:S(2)}) collective-permute-start(bf16[2,256,128]{2,1,0:T(8,128)(2,1)S(1)} %get-tuple-element.19), channel_id=1, source_target_pairs={{0,16},{2,18},{4,20},{6,22},{8,24},{10,26},{12,28},{14,30},{16,0},... | collective-permute-start | bytes 393224 | tf_op jit(solution)/shard_map/ppermute | solution.py:383
  35.7 3.4 %all-to-all-start.1 = ((bf16[392,2,128]{2,1,0:T(2,128)(2,1)}), bf16[392,2,128]{2,1,0:T(2,128)(2,1)S(1)}, u32[]{:S(2)}, u32[]{:S(2)}) async-start(bf16[392,2,128]{2,1,0:T(2,128)(2,1)} %get-tuple-element.17), calls=%async_computation.1 | async-start | bytes 401408 | tf_op jit(solution)/shard_map/all_to_all | solution.py:380
  39.1 3.2 %collective-permute-done = bf16[2,256,128]{2,1,0:T(8,128)(2,1)S(1)} collective-permute-done((bf16[2,256,128]{2,1,0:T(8,128)(2,1)S(1)}, bf16[2,256,128]{2,1,0:T(8,128)(2,1)S(1)}, u32[]{:S(2)}, u32[]{:S(2)}) %collective-permute-start) | collective-permute-done | bytes 131104 | tf_op jit(solution)/shard_map/ppermute | solution.py:383
  42.3 5.6 %all-gather.1 = bf16[4,256,128]{2,1,0:T(8,128)(2,1)S(1)} all-gather(bf16[2,256,128]{2,1,0:T(8,128)(2,1)S(1)} %add_convert_fusion), channel_id=3, replica_groups=mesh['tile'=16,'freq'=2] {'freq'}, dimensions={0}, use_global_device_ids=true | all-gather | bytes 393216 | tf_op jit(solution)/shard_map/all_gather | solution.py:384
  48.0 0.0 all-to-all-done.1.returned_ref
  48.0 1.6 %finish.1 = (f32[128,2,128]{2,1,0:T(2,128)}, f32[2,128,256]{2,1,0:T(8,128)}) custom-call(f32[2]{0:T(128)S(1)} %dynamic-slice_bitcast_fusion.row_ref, s32[128]{0:T(128)S(1)} %broadcast_add_fusion.slot_ref, bf16[392,2,128]{2,1,0:T(2,128)(2,1)S(1)} %all-to-all-done.1.returned_ref, bf16[2,2,256,128]{3,2,1,0:T(8,128)(2,1)S(1)} %bitcast.20), custom_call_target="tpu_custom_call" | custom-call | tf_op jit(solution)/shard_map/finish/pallas_call | solution.py:385
  (5 shorter events, 0.1 us)
Async XLA Ops:
  0.6 19.3 %copy-start = (f32[2,2]{1,0:T(2,128)S(1)}, f32[2,2]{1,0:T(2,128)}, u32[]{:S(2)}) copy-start(f32[2,2]{1,0:T(2,128)} %param.15) | copy-start | bytes 52
  4.0 18.0 %all-to-all-start = ((s32[8,152,128]{2,1,0:T(8,128)}), s32[8,152,128]{2,1,0:T(8,128)S(1)}, u32[]{:S(2)}, u32[]{:S(2)}) async-start(s32[8,152,128]{2,1,0:T(8,128)} %bitcast.21), calls=%async_computation | async-start | bytes 1245184 | tf_op jit(solution)/shard_map/all_to_all | solution.py:345
  9.3 0.7 %copy-start.2 = (bf16[16,8,8]{0,2,1:T(8,128)(2,1)S(1)}, bf16[16,8,8]{0,2,1:T(8,128)(2,1)}, u32[]{:S(2)}) copy-start(bf16[16,8,8]{0,2,1:T(8,128)(2,1)} %param.14) | copy-start | bytes 6148
  9.3 0.9 %copy-start.1 = (bf16[1,2,128,256]{3,2,1,0:T(8,128)(2,1)S(1)}, bf16[1,2,128,256]{3,2,1,0:T(8,128)(2,1)}, u32[]{:S(2)}) copy-start(bf16[1,2,128,256]{3,2,1,0:T(8,128)(2,1)} %param.13) | copy-start | bytes 393220
  20.0 0.7 %copy-start.3 = (s32[128]{0:T(128)S(1)}, s32[128]{0:T(128)}, u32[]{:S(2)}) copy-start(s32[128]{0:T(128)} %get-tuple-element.12) | copy-start | bytes 1540
  33.5 8.7 %collective-permute-start = (bf16[2,256,128]{2,1,0:T(8,128)(2,1)S(1)}, bf16[2,256,128]{2,1,0:T(8,128)(2,1)S(1)}, u32[]{:S(2)}, u32[]{:S(2)}) collective-permute-start(bf16[2,256,128]{2,1,0:T(8,128)(2,1)S(1)} %get-tuple-element.19), channel_id=1, source_target_pairs={{0,16},{2,18},{4,20},{6,22},{8,24},{10,26},{12,28},{14,30},{16,0},... | collective-permute-start | bytes 393224 | tf_op jit(solution)/shard_map/ppermute | solution.py:383
  35.7 12.3 %all-to-all-start.1 = ((bf16[392,2,128]{2,1,0:T(2,128)(2,1)}), bf16[392,2,128]{2,1,0:T(2,128)(2,1)S(1)}, u32[]{:S(2)}, u32[]{:S(2)}) async-start(bf16[392,2,128]{2,1,0:T(2,128)(2,1)} %get-tuple-element.17), calls=%async_computation.1 | async-start | bytes 401408 | tf_op jit(solution)/shard_map/all_to_all | solution.py:380
where the time goes:
time: 48.7 us; the launch traced here: 49.6 us
  Pallas kernels  16.5 us (34%)
  blocking collectives  15.4 us (32%)
  starting transfers between devices  10.8 us (22%)
  waiting for transfers between devices  4.6 us (9%)
  local copies, waits for them, and re-layouts  1.55 us (3%)
  between operations  0.7 us (1%)
    pallas_call x1, Pallas kernels, body(): pl.pallas_call(lambda *refs: grid_kernel(pairs, capacity, *refs), out_sha...  11.5 us
    all_gather x1, blocking collectives, body(): lax.all_gather(model_grid[0], 'tile', axis=0, tiled=True, axis_index_grou...  9.71 us
    all_gather x1, blocking collectives, body(): lax.all_gather(grid_sum.astype(jnp.bfloat16)[None], 'freq', axis=0, tiled...  5.64 us
    all_to_all x1, starting transfers between devices, body(): lax.all_to_all(sent, 'tile', split_axis=0, concat_axis=0, tiled=True, axi...  5.27 us
    pallas_call x1, Pallas kernels, body(): pl.pallas_call(lambda *refs: pack_kernel(pairs, capacity, tiles_here, *re...  3.4 us
    all_to_all x1, starting transfers between devices, body(): lax.all_to_all(residual, 'tile', split_axis=0, concat_axis=0, tiled=True,...  3.39 us
    ppermute x1, waiting for transfers between devices, body(): grid_sum = own + lax.ppermute(other, 'tile', swap).astype(jnp.float32)  3.19 us
    ppermute x1, starting transfers between devices, body(): grid_sum = own + lax.ppermute(other, 'tile', swap).astype(jnp.float32)  2.15 us
  transfers between devices with their start and end apart: 3, of which 2 were waited for; matrix products, arithmetic and copies ran while one was open for 0% of the time, Pallas kernels for 0%

commit v1 on v0

--- a/solution.py
+++ b/solution.py
@@ -7,7 +7,7 @@
 
 UNROLL = 2
 CHUNKS = 35
-AHEAD = 2
+AHEAD = 3
 BUFFERS = 5
 VMEM = pl.BlockSpec(memory_space=pltpu.VMEM)
 SMEM = pl.BlockSpec(memory_space=pltpu.SMEM)
@@ -118,12 +118,14 @@
         sent_ref[row + 2 : row + 3, :] = counts
 
 
-def finish_kernel(row_ref, slot_ref, returned_ref, grid_ref, residual_ref, coupled_ref):
+def finish_kernel(row_ref, slot_ref, returned_ref, grid_ref, residual_ref, coupled_hbm, coupled_ref, sem):
     planes, tiles_here = grid_ref.shape[:2]
     for t in range(tiles_here):
         coupled_ref[t] = sum(
             row_ref[g] * grid_ref[g, t].astype(jnp.float32) for g in range(planes)
         ).T
+    leave = pltpu.make_async_copy(coupled_ref, coupled_hbm, sem)
+    leave.start()
 
     def step(turn, carry):
         for which in range(8):
@@ -132,6 +134,7 @@
         return carry
 
     lax.fori_loop(0, residual_ref.shape[0] // 8, step, 0)
+    leave.wait()
 
 
 def spread_parts(start, offset, table):
@@ -389,7 +392,11 @@
             jax.ShapeDtypeStruct((tiles_here, side, wide), jnp.float32),
         ),
         in_specs=[SMEM, SMEM, VMEM, VMEM],
-        out_specs=(VMEM, VMEM),
+        out_specs=(VMEM, HBM),
+        scratch_shapes=[
+            pltpu.VMEM((tiles_here, side, wide), jnp.float32),
+            pltpu.SemaphoreType.DMA,
+        ],
         compiler_params=PARAMS,
         name="finish",
     )(own_row, slot, returned, grids)

time: 48.7 us -> 48.8 us (level); the launches traced: 49.6 us -> 48.1 us
  starting transfers between devices: 10.8 us -> 17 us
  Pallas kernels: 16.5 us -> 11 us
  waiting for transfers between devices: 4.6 us -> 1.41 us
  blocking collectives: 15.4 us -> 16.3 us
    all_to_all x1, starting transfers between devices: 3.39 us -> 9.62 us  [body(): lax.all_to_all(residual, 'tile', split_axis=0, concat_axis=0, tiled=True,...]
    pallas_call x1, Pallas kernels: 11.5 us -> 5.58 us  [body(): pl.pallas_call(lambda *refs: grid_kernel(pairs, capacity, *refs), out_sha...]
    ppermute x1, waiting for transfers between devices: 3.19 us -> 0.01 us  [body(): grid_sum = own + lax.ppermute(other, 'tile', swap).astype(jnp.float32)]
    all_gather x1, blocking collectives: 5.64 us -> 6.58 us  [body(): lax.all_gather(grid_sum.astype(jnp.bfloat16)[None], 'freq', axis=0, tiled...]
  transfers between devices with their start and end apart: 3 -> 3, of which waited for: 2 -> 1; matrix products, arithmetic and copies ran while one was open for 0% -> 0% of each run, Pallas kernels for 0% -> 0%
where the time goes in v1:
time: 48.8 us; the launch traced here: 48.1 us
  starting transfers between devices  17 us (35%)
  blocking collectives  16.3 us (33%)
  Pallas kernels  11 us (23%)
  local copies, waits for them, and re-layouts  1.55 us (3%)
  waiting for transfers between devices  1.41 us (3%)
  between operations  0.7 us (1%)
    all_gather x1, blocking collectives, body(): lax.all_gather(model_grid[0], 'tile', axis=0, tiled=True, axis_index_grou...  9.71 us
    all_to_all x1, starting transfers between devices, body(): lax.all_to_all(residual, 'tile', split_axis=0, concat_axis=0, tiled=True,...  9.62 us
    all_gather x1, blocking collectives, body(): lax.all_gather(grid_sum.astype(jnp.bfloat16)[None], 'freq', axis=0, tiled...  6.58 us
    pallas_call x1, Pallas kernels, body(): pl.pallas_call(lambda *refs: grid_kernel(pairs, capacity, *refs), out_sha...  5.58 us
    all_to_all x1, starting transfers between devices, body(): lax.all_to_all(sent, 'tile', split_axis=0, concat_axis=0, tiled=True, axi...  5.27 us
    pallas_call x1, Pallas kernels, body(): pl.pallas_call(lambda *refs: pack_kernel(pairs, capacity, tiles_here, *re...  3.4 us
    ppermute x1, starting transfers between devices, body(): grid_sum = own + lax.ppermute(other, 'tile', swap).astype(jnp.float32)  2.15 us
    pallas_call x1, Pallas kernels, body(): pl.pallas_call(finish_kernel, out_shape=(jax.ShapeDtypeStruct((blocks, 2,...  2.05 us
  transfers between devices with their start and end apart: 3, of which 1 were waited for; matrix products, arithmetic and copies ran while one was open for 0% of the time, Pallas kernels for 0%

profile of v1, /device:TPU:0, one launch (start us, length us, event | category | flops | bytes accessed | tf_op | source)
XLA Modules:
  0.0 48.1 jit_solution(1302056867004028127)
XLA Ops:
  0.6 0.0 copy-start
  0.6 3.4 %pack_blocks.1 = (s32[1216,128]{1,0:T(8,128)}, s32[128]{0:T(128)}) custom-call(s32[128]{0:T(128)} %bitcast.26, s32[128]{0:T(128)} %bitcast.27, f32[256,128]{1,0:T(8,128)} %bitcast.22, s32[256,128]{1,0:T(8,128)} %bitcast.23, s32[256,128]{1,0:T(8,128)} %bitcast.24), custom_call_target="tpu_custom_call" | custom-call | tf_op jit(solution)/shard_map/pack_blocks/pallas_call | solution.py:322
  4.0 5.3 %all-to-all-start = ((s32[8,152,128]{2,1,0:T(8,128)}), s32[8,152,128]{2,1,0:T(8,128)S(1)}, u32[]{:S(2)}, u32[]{:S(2)}) async-start(s32[8,152,128]{2,1,0:T(8,128)} %bitcast.21), calls=%async_computation | async-start | bytes 1245184 | tf_op jit(solution)/shard_map/all_to_all | solution.py:348
  9.3 0.0 copy-start.2
  9.3 0.0 copy-start.1
  9.3 0.7 %copy-done.2 = bf16[16,8,8]{0,2,1:T(8,128)(2,1)S(1)} copy-done((bf16[16,8,8]{0,2,1:T(8,128)(2,1)S(1)}, bf16[16,8,8]{0,2,1:T(8,128)(2,1)}, u32[]{:S(2)}) %copy-start.2) | copy-done | bytes 2072
  10.1 0.1 copy.14.refs_2_
  10.1 0.1 copy-done.1
  10.2 9.7 %all-gather = bf16[1,4,128,256]{3,2,0,1:T(8,128)(2,1)S(1)} all-gather(bf16[1,2,128,256]{3,2,0,1:T(8,128)(2,1)S(1)} %bitcast.25), channel_id=2, replica_groups={{0,16},{2,18},{4,20},{6,22},{8,24},{10,26},{12,28},{14,30},{1,17},{3,19..., dimensions={1}, use_global_device_ids=true | all-gather | bytes 393216 | tf_op jit(solution)/shard_map/all_gather | solution.py:315
  19.9 0.0 copy-done
  20.0 0.0 copy-start.3
  20.0 0.6 %copy-done.3 = s32[128]{0:T(128)S(1)} copy-done((s32[128]{0:T(128)S(1)}, s32[128]{0:T(128)}, u32[]{:S(2)}) %copy-start.3) | copy-done | bytes 536
  20.6 1.4 %all-to-all-done = s32[8,152,128]{2,1,0:T(8,128)S(1)} async-done(((s32[8,152,128]{2,1,0:T(8,128)}), s32[8,152,128]{2,1,0:T(8,128)S(1)}, u32[]{:S(2)}, u32[]{:S(2)}) %all-to-all-start) | async-done | bytes 622624 | tf_op jit(solution)/shard_map/all_to_all | solution.py:348
  22.0 5.6 %grid_blocks.1 = (bf16[392,2,128]{2,1,0:T(2,128)(2,1)}, f32[2,256,128]{2,1,0:T(8,128)S(1)}, bf16[2,256,128]{2,1,0:T(8,128)(2,1)S(1)}) custom-call(s32[1]{0:T(128)} %bitcast.8.refs_0_, s32[1216,128]{1,0:T(8,128)S(1)} %bitcast.18, f32[24,128]{1,0:T(8,128)S(1)} %copy.14.refs_2_, bf16[4,128,256]{2,1,0:T(8,128)(2,1)S(1)} %bitcast.19), custom_call_target="tpu_custom_call" | custom-call | tf_op jit(solution)/shard_map/grid_blocks/pallas_call | solution.py:358
  27.6 2.1 %collective-permute-start = (bf16[2,256,128]{2,1,0:T(8,128)(2,1)S(1)}, bf16[2,256,128]{2,1,0:T(8,128)(2,1)S(1)}, u32[]{:S(2)}, u32[]{:S(2)}) collective-permute-start(bf16[2,256,128]{2,1,0:T(8,128)(2,1)S(1)} %get-tuple-element.19), channel_id=1, source_target_pairs={{0,16},{2,18},{4,20},{6,22},{8,24},{10,26},{12,28},{14,30},{16,0},... | collective-permute-start | bytes 393224 | tf_op jit(solution)/shard_map/ppermute | solution.py:386
  29.8 9.6 %all-to-all-start.1 = ((bf16[392,2,128]{2,1,0:T(2,128)(2,1)}), bf16[392,2,128]{2,1,0:T(2,128)(2,1)S(1)}, u32[]{:S(2)}, u32[]{:S(2)}) async-start(bf16[392,2,128]{2,1,0:T(2,128)(2,1)} %get-tuple-element.17), calls=%async_computation.1 | async-start | bytes 401408 | tf_op jit(solution)/shard_map/all_to_all | solution.py:383
  39.4 0.0 collective-permute-done
  39.4 6.6 %all-gather.1 = bf16[4,256,128]{2,1,0:T(8,128)(2,1)S(1)} all-gather(bf16[2,256,128]{2,1,0:T(8,128)(2,1)S(1)} %add_convert_fusion), channel_id=3, replica_groups=mesh['tile'=16,'freq'=2] {'freq'}, dimensions={0}, use_global_device_ids=true | all-gather | bytes 393216 | tf_op jit(solution)/shard_map/all_gather | solution.py:387
  46.0 0.0 all-to-all-done.1.returned_ref
  46.0 2.0 %finish.1 = (f32[128,2,128]{2,1,0:T(2,128)}, f32[2,128,256]{2,1,0:T(8,128)}) custom-call(f32[2]{0:T(128)S(1)} %dynamic-slice_bitcast_fusion.row_ref, s32[128]{0:T(128)S(1)} %broadcast_add_fusion.slot_ref, bf16[392,2,128]{2,1,0:T(2,128)(2,1)S(1)} %all-to-all-done.1.returned_ref, bf16[2,2,256,128]{3,2,1,0:T(8,128)(2,1)S(1)} %bitcast.20), custom_call_target="tpu_custom_call" | custom-call | tf_op jit(solution)/shard_map/finish/pallas_call | solution.py:388
  (5 shorter events, 0.1 us)
Async XLA Ops:
  0.6 19.3 %copy-start = (f32[2,2]{1,0:T(2,128)S(1)}, f32[2,2]{1,0:T(2,128)}, u32[]{:S(2)}) copy-start(f32[2,2]{1,0:T(2,128)} %param.15) | copy-start | bytes 52
  4.0 18.0 %all-to-all-start = ((s32[8,152,128]{2,1,0:T(8,128)}), s32[8,152,128]{2,1,0:T(8,128)S(1)}, u32[]{:S(2)}, u32[]{:S(2)}) async-start(s32[8,152,128]{2,1,0:T(8,128)} %bitcast.21), calls=%async_computation | async-start | bytes 1245184 | tf_op jit(solution)/shard_map/all_to_all | solution.py:348
  9.3 0.7 %copy-start.2 = (bf16[16,8,8]{0,2,1:T(8,128)(2,1)S(1)}, bf16[16,8,8]{0,2,1:T(8,128)(2,1)}, u32[]{:S(2)}) copy-start(bf16[16,8,8]{0,2,1:T(8,128)(2,1)} %param.14) | copy-start | bytes 6148
  9.3 0.9 %copy-start.1 = (bf16[1,2,128,256]{3,2,1,0:T(8,128)(2,1)S(1)}, bf16[1,2,128,256]{3,2,1,0:T(8,128)(2,1)}, u32[]{:S(2)}) copy-start(bf16[1,2,128,256]{3,2,1,0:T(8,128)(2,1)} %param.13) | copy-start | bytes 393220
  20.0 0.7 %copy-start.3 = (s32[128]{0:T(128)S(1)}, s32[128]{0:T(128)}, u32[]{:S(2)}) copy-start(s32[128]{0:T(128)} %get-tuple-element.12) | copy-start | bytes 1540
  27.6 11.8 %collective-permute-start = (bf16[2,256,128]{2,1,0:T(8,128)(2,1)S(1)}, bf16[2,256,128]{2,1,0:T(8,128)(2,1)S(1)}, u32[]{:S(2)}, u32[]{:S(2)}) collective-permute-start(bf16[2,256,128]{2,1,0:T(8,128)(2,1)S(1)} %get-tuple-element.19), channel_id=1, source_target_pairs={{0,16},{2,18},{4,20},{6,22},{8,24},{10,26},{12,28},{14,30},{16,0},... | collective-permute-start | bytes 393224 | tf_op jit(solution)/shard_map/ppermute | solution.py:386
  29.8 16.2 %all-to-all-start.1 = ((bf16[392,2,128]{2,1,0:T(2,128)(2,1)}), bf16[392,2,128]{2,1,0:T(2,128)(2,1)S(1)}, u32[]{:S(2)}, u32[]{:S(2)}) async-start(bf16[392,2,128]{2,1,0:T(2,128)(2,1)} %get-tuple-element.17), calls=%async_computation.1 | async-start | bytes 401408 | tf_op jit(solution)/shard_map/all_to_all | solution.py:383

commit v2 on v0

--- a/solution.py
+++ b/solution.py
@@ -148,7 +148,7 @@
 
 def grid_kernel(pairs, capacity, member_ref, got_ref, table_ref, model_ref, residual_ref, own_ref,
                 other_ref, turned_ref, grid_ref, code_ref, about_ref, list_ref, sem, *buffers):
-    row_refs, picked_refs = buffers[:BUFFERS], buffers[BUFFERS:]
+    row_refs, kept_refs = buffers[:BUFFERS], buffers[BUFFERS:]
     tiles, side, wide = model_ref.shape
     groups = side // 16
     zero_row = table_ref.shape[0] - 8
@@ -232,7 +232,7 @@
         return (list_ref[turn * UNROLL] >> TILE_SHIFT) & 15
 
     def front(turn, which):
-        row_ref, picked_ref = row_refs[which % len(row_refs)], picked_refs[which % len(picked_refs)]
+        row_ref, kept_ref = row_refs[which % len(row_refs)], kept_refs[which % len(kept_refs)]
         blocks = [read(turn * UNROLL + u) for u in range(UNROLL)]
         matrices = []
         for _, _, parts in blocks:
@@ -247,32 +247,32 @@
         partial = jnp.dot(
             turned_ref[chunk_tile(turn)], row_matrix, preferred_element_type=jnp.float32
         )
-        for u, (_, _, parts) in enumerate(blocks):
+        for u, (slot, sample, parts) in enumerate(blocks):
             columns = slice(128 * u, 128 * u + 128)
             taps, group = parts(0)
+            residuals = []
             for part in range(2):
                 picked = jnp.zeros((16, 128), jnp.float32)
                 for k in range(groups):
                     low = part * side + 16 * k
                     picked = jnp.where(group == k, partial[low : low + 16, columns], picked)
-                picked_ref[part, :, columns] = picked * taps
+                model = jnp.sum(picked * taps, axis=0, keepdims=True)
+                residuals.append(sample(part) - model)
+                kept_ref[part : part + 1, columns] = residuals[part]
+            residual_ref[slot] = jnp.concatenate(residuals, axis=0).astype(jnp.bfloat16)
 
     def back(turn, which):
-        row_ref, picked_ref = row_refs[which % len(row_refs)], picked_refs[which % len(picked_refs)]
+        row_ref, kept_ref = row_refs[which % len(row_refs)], kept_refs[which % len(kept_refs)]
         weighted = []
         for u in range(UNROLL):
-            slot, sample, parts = read(turn * UNROLL + u)
+            _, _, parts = read(turn * UNROLL + u)
             columns = slice(128 * u, 128 * u + 128)
             taps, group = parts(0)
             group = group.astype(jnp.float32).astype(jnp.bfloat16)
-            residuals, pieces = [], []
+            pieces = []
             for part in range(2):
-                model = jnp.sum(picked_ref[part, :, columns], axis=0, keepdims=True)
-                residual = sample(part) - model
-                residuals.append(residual)
-                value = (residual * taps).astype(jnp.bfloat16)
+                value = (kept_ref[part : part + 1, columns] * taps).astype(jnp.bfloat16)
                 pieces += [jnp.where(group == k, value, zero) for k in range(groups)]
-            residual_ref[slot] = jnp.concatenate(residuals, axis=0).astype(jnp.bfloat16)
             weighted.append(jnp.concatenate(pieces, axis=0))
         grid_ref[chunk_tile(turn)] += lax.dot_general(
             jnp.concatenate(weighted, axis=1),
@@ -371,7 +371,7 @@
             ),
             pltpu.SemaphoreType.DMA,
             *[pltpu.VMEM((side, UNROLL * rows), jnp.bfloat16)] * BUFFERS,
-            *[pltpu.VMEM((2, 16, UNROLL * rows), jnp.float32)] * BUFFERS,
+            *[pltpu.VMEM((8, UNROLL * rows), jnp.float32)] * BUFFERS,
         ],
         compiler_params=PARAMS,
         name="grid_blocks",

time: 48.7 us -> 48 us (0.986); the launches traced: 49.6 us -> 47.3 us
  waiting for transfers between devices: 4.6 us -> 1.97 us
    ppermute x1, waiting for transfers between devices: 3.19 us -> 0.56 us  [body(): grid_sum = own + lax.ppermute(other, 'tile', swap).astype(jnp.float32)]
where the time goes in v2:
time: 48 us; the launch traced here: 47.3 us
  Pallas kernels  16.6 us (35%)
  blocking collectives  15.6 us (32%)
  starting transfers between devices  10.8 us (22%)
  waiting for transfers between devices  1.97 us (4%)
  local copies, waits for them, and re-layouts  1.55 us (3%)
  between operations  0.7 us (1%)
    pallas_call x1, Pallas kernels, body(): pl.pallas_call(lambda *refs: grid_kernel(pairs, capacity, *refs), out_sha...  11.7 us
    all_gather x1, blocking collectives, body(): lax.all_gather(model_grid[0], 'tile', axis=0, tiled=True, axis_index_grou...  9.71 us
    all_gather x1, blocking collectives, body(): lax.all_gather(grid_sum.astype(jnp.bfloat16)[None], 'freq', axis=0, tiled...  5.93 us
    all_to_all x1, starting transfers between devices, body(): lax.all_to_all(sent, 'tile', split_axis=0, concat_axis=0, tiled=True, axi...  5.27 us
    pallas_call x1, Pallas kernels, body(): pl.pallas_call(lambda *refs: pack_kernel(pairs, capacity, tiles_here, *re...  3.4 us
    all_to_all x1, starting transfers between devices, body(): lax.all_to_all(residual, 'tile', split_axis=0, concat_axis=0, tiled=True,...  3.39 us
    ppermute x1, starting transfers between devices, body(): grid_sum = own + lax.ppermute(other, 'tile', swap).astype(jnp.float32)  2.09 us
    pallas_call x1, Pallas kernels, body(): pl.pallas_call(finish_kernel, out_shape=(jax.ShapeDtypeStruct((blocks, 2,...  1.6 us
  transfers between devices with their start and end apart: 3, of which 2 were waited for; matrix products, arithmetic and copies ran while one was open for 0% of the time, Pallas kernels for 0%

profile of v2, /device:TPU:0, one launch (start us, length us, event | category | flops | bytes accessed | tf_op | source)
XLA Modules:
  0.0 47.3 jit_solution(14882463090758586894)
XLA Ops:
  0.6 0.0 copy-start
  0.6 3.4 %pack_blocks.1 = (s32[1216,128]{1,0:T(8,128)}, s32[128]{0:T(128)}) custom-call(s32[128]{0:T(128)} %bitcast.26, s32[128]{0:T(128)} %bitcast.27, f32[256,128]{1,0:T(8,128)} %bitcast.22, s32[256,128]{1,0:T(8,128)} %bitcast.23, s32[256,128]{1,0:T(8,128)} %bitcast.24), custom_call_target="tpu_custom_call" | custom-call | tf_op jit(solution)/shard_map/pack_blocks/pallas_call | solution.py:319
  4.0 5.3 %all-to-all-start = ((s32[8,152,128]{2,1,0:T(8,128)}), s32[8,152,128]{2,1,0:T(8,128)S(1)}, u32[]{:S(2)}, u32[]{:S(2)}) async-start(s32[8,152,128]{2,1,0:T(8,128)} %bitcast.21), calls=%async_computation | async-start | bytes 1245184 | tf_op jit(solution)/shard_map/all_to_all | solution.py:345
  9.3 0.0 copy-start.2
  9.3 0.0 copy-start.1
  9.3 0.7 %copy-done.2 = bf16[16,8,8]{0,2,1:T(8,128)(2,1)S(1)} copy-done((bf16[16,8,8]{0,2,1:T(8,128)(2,1)S(1)}, bf16[16,8,8]{0,2,1:T(8,128)(2,1)}, u32[]{:S(2)}) %copy-start.2) | copy-done | bytes 2072
  10.1 0.1 copy.14.refs_2_
  10.1 0.1 copy-done.1
  10.2 9.7 %all-gather = bf16[1,4,128,256]{3,2,0,1:T(8,128)(2,1)S(1)} all-gather(bf16[1,2,128,256]{3,2,0,1:T(8,128)(2,1)S(1)} %bitcast.25), channel_id=2, replica_groups={{0,16},{2,18},{4,20},{6,22},{8,24},{10,26},{12,28},{14,30},{1,17},{3,19..., dimensions={1}, use_global_device_ids=true | all-gather | bytes 393216 | tf_op jit(solution)/shard_map/all_gather | solution.py:312
  19.9 0.0 copy-done
  20.0 0.0 copy-start.3
  20.0 0.6 %copy-done.3 = s32[128]{0:T(128)S(1)} copy-done((s32[128]{0:T(128)S(1)}, s32[128]{0:T(128)}, u32[]{:S(2)}) %copy-start.3) | copy-done | bytes 536
  20.6 1.4 %all-to-all-done = s32[8,152,128]{2,1,0:T(8,128)S(1)} async-done(((s32[8,152,128]{2,1,0:T(8,128)}), s32[8,152,128]{2,1,0:T(8,128)S(1)}, u32[]{:S(2)}, u32[]{:S(2)}) %all-to-all-start) | async-done | bytes 622624 | tf_op jit(solution)/shard_map/all_to_all | solution.py:345
  22.0 11.7 %grid_blocks.1 = (bf16[392,2,128]{2,1,0:T(2,128)(2,1)}, f32[2,256,128]{2,1,0:T(8,128)S(1)}, bf16[2,256,128]{2,1,0:T(8,128)(2,1)S(1)}) custom-call(s32[1]{0:T(128)} %bitcast.8.refs_0_, s32[1216,128]{1,0:T(8,128)S(1)} %bitcast.18, f32[24,128]{1,0:T(8,128)S(1)} %copy.14.refs_2_, bf16[4,128,256]{2,1,0:T(8,128)(2,1)S(1)} %bitcast.19), custom_call_target="tpu_custom_call" | custom-call | tf_op jit(solution)/shard_map/grid_blocks/pallas_call | solution.py:355
  33.7 2.1 %collective-permute-start = (bf16[2,256,128]{2,1,0:T(8,128)(2,1)S(1)}, bf16[2,256,128]{2,1,0:T(8,128)(2,1)S(1)}, u32[]{:S(2)}, u32[]{:S(2)}) collective-permute-start(bf16[2,256,128]{2,1,0:T(8,128)(2,1)S(1)} %get-tuple-element.19), channel_id=1, source_target_pairs={{0,16},{2,18},{4,20},{6,22},{8,24},{10,26},{12,28},{14,30},{16,0},... | collective-permute-start | bytes 393224 | tf_op jit(solution)/shard_map/ppermute | solution.py:383
  35.8 3.4 %all-to-all-start.1 = ((bf16[392,2,128]{2,1,0:T(2,128)(2,1)}), bf16[392,2,128]{2,1,0:T(2,128)(2,1)S(1)}, u32[]{:S(2)}, u32[]{:S(2)}) async-start(bf16[392,2,128]{2,1,0:T(2,128)(2,1)} %get-tuple-element.17), calls=%async_computation.1 | async-start | bytes 401408 | tf_op jit(solution)/shard_map/all_to_all | solution.py:380
  39.2 0.6 %collective-permute-done = bf16[2,256,128]{2,1,0:T(8,128)(2,1)S(1)} collective-permute-done((bf16[2,256,128]{2,1,0:T(8,128)(2,1)S(1)}, bf16[2,256,128]{2,1,0:T(8,128)(2,1)S(1)}, u32[]{:S(2)}, u32[]{:S(2)}) %collective-permute-start) | collective-permute-done | bytes 131104 | tf_op jit(solution)/shard_map/ppermute | solution.py:383
  39.8 5.9 %all-gather.1 = bf16[4,256,128]{2,1,0:T(8,128)(2,1)S(1)} all-gather(bf16[2,256,128]{2,1,0:T(8,128)(2,1)S(1)} %add_convert_fusion), channel_id=3, replica_groups=mesh['tile'=16,'freq'=2] {'freq'}, dimensions={0}, use_global_device_ids=true | all-gather | bytes 393216 | tf_op jit(solution)/shard_map/all_gather | solution.py:384
  45.7 0.0 all-to-all-done.1.returned_ref
  45.7 1.6 %finish.1 = (f32[128,2,128]{2,1,0:T(2,128)}, f32[2,128,256]{2,1,0:T(8,128)}) custom-call(f32[2]{0:T(128)S(1)} %dynamic-slice_bitcast_fusion.row_ref, s32[128]{0:T(128)S(1)} %broadcast_add_fusion.slot_ref, bf16[392,2,128]{2,1,0:T(2,128)(2,1)S(1)} %all-to-all-done.1.returned_ref, bf16[2,2,256,128]{3,2,1,0:T(8,128)(2,1)S(1)} %bitcast.20), custom_call_target="tpu_custom_call" | custom-call | tf_op jit(solution)/shard_map/finish/pallas_call | solution.py:385
  (5 shorter events, 0.1 us)
Async XLA Ops:
  0.6 19.3 %copy-start = (f32[2,2]{1,0:T(2,128)S(1)}, f32[2,2]{1,0:T(2,128)}, u32[]{:S(2)}) copy-start(f32[2,2]{1,0:T(2,128)} %param.15) | copy-start | bytes 52
  4.0 18.0 %all-to-all-start = ((s32[8,152,128]{2,1,0:T(8,128)}), s32[8,152,128]{2,1,0:T(8,128)S(1)}, u32[]{:S(2)}, u32[]{:S(2)}) async-start(s32[8,152,128]{2,1,0:T(8,128)} %bitcast.21), calls=%async_computation | async-start | bytes 1245184 | tf_op jit(solution)/shard_map/all_to_all | solution.py:345
  9.3 0.7 %copy-start.2 = (bf16[16,8,8]{0,2,1:T(8,128)(2,1)S(1)}, bf16[16,8,8]{0,2,1:T(8,128)(2,1)}, u32[]{:S(2)}) copy-start(bf16[16,8,8]{0,2,1:T(8,128)(2,1)} %param.14) | copy-start | bytes 6148
  9.3 0.9 %copy-start.1 = (bf16[1,2,128,256]{3,2,1,0:T(8,128)(2,1)S(1)}, bf16[1,2,128,256]{3,2,1,0:T(8,128)(2,1)}, u32[]{:S(2)}) copy-start(bf16[1,2,128,256]{3,2,1,0:T(8,128)(2,1)} %param.13) | copy-start | bytes 393220
  20.0 0.7 %copy-start.3 = (s32[128]{0:T(128)S(1)}, s32[128]{0:T(128)}, u32[]{:S(2)}) copy-start(s32[128]{0:T(128)} %get-tuple-element.12) | copy-start | bytes 1540
  33.7 6.1 %collective-permute-start = (bf16[2,256,128]{2,1,0:T(8,128)(2,1)S(1)}, bf16[2,256,128]{2,1,0:T(8,128)(2,1)S(1)}, u32[]{:S(2)}, u32[]{:S(2)}) collective-permute-start(bf16[2,256,128]{2,1,0:T(8,128)(2,1)S(1)} %get-tuple-element.19), channel_id=1, source_target_pairs={{0,16},{2,18},{4,20},{6,22},{8,24},{10,26},{12,28},{14,30},{16,0},... | collective-permute-start | bytes 393224 | tf_op jit(solution)/shard_map/ppermute | solution.py:383
  35.8 9.9 %all-to-all-start.1 = ((bf16[392,2,128]{2,1,0:T(2,128)(2,1)}), bf16[392,2,128]{2,1,0:T(2,128)(2,1)S(1)}, u32[]{:S(2)}, u32[]{:S(2)}) async-start(bf16[392,2,128]{2,1,0:T(2,128)(2,1)} %get-tuple-element.17), calls=%async_computation.1 | async-start | bytes 401408 | tf_op jit(solution)/shard_map/all_to_all | solution.py:380

commit v3 on v0

--- a/solution.py
+++ b/solution.py
@@ -126,12 +126,12 @@
         ).T
 
     def step(turn, carry):
-        for which in range(8):
-            b = turn * 8 + which
+        for which in range(32):
+            b = turn * 32 + which
             residual_ref[b] = returned_ref[slot_ref[b]].astype(jnp.float32)
         return carry
 
-    lax.fori_loop(0, residual_ref.shape[0] // 8, step, 0)
+    lax.fori_loop(0, residual_ref.shape[0] // 32, step, 0)
 
 
 def spread_parts(start, offset, table):

time: 48.7 us -> 48.1 us (0.988); the launches traced: 49.6 us -> 47.3 us
  waiting for transfers between devices: 4.6 us -> 1.69 us
  blocking collectives: 15.4 us -> 16 us
    ppermute x1, waiting for transfers between devices: 3.19 us -> 0.28 us  [body(): grid_sum = own + lax.ppermute(other, 'tile', swap).astype(jnp.float32)]
    all_gather x1, blocking collectives: 5.64 us -> 6.31 us  [body(): lax.all_gather(grid_sum.astype(jnp.bfloat16)[None], 'freq', axis=0, tiled...]
where the time goes in v3:
time: 48.1 us; the launch traced here: 47.3 us
  Pallas kernels  16.3 us (34%)
  blocking collectives  16 us (33%)
  starting transfers between devices  11 us (23%)
  waiting for transfers between devices  1.69 us (4%)
  local copies, waits for them, and re-layouts  1.55 us (3%)
  between operations  0.7 us (1%)
    pallas_call x1, Pallas kernels, body(): pl.pallas_call(lambda *refs: grid_kernel(pairs, capacity, *refs), out_sha...  11.3 us
    all_gather x1, blocking collectives, body(): lax.all_gather(model_grid[0], 'tile', axis=0, tiled=True, axis_index_grou...  9.71 us
    all_gather x1, blocking collectives, body(): lax.all_gather(grid_sum.astype(jnp.bfloat16)[None], 'freq', axis=0, tiled...  6.31 us
    all_to_all x1, starting transfers between devices, body(): lax.all_to_all(sent, 'tile', split_axis=0, concat_axis=0, tiled=True, axi...  5.27 us
    all_to_all x1, starting transfers between devices, body(): lax.all_to_all(residual, 'tile', split_axis=0, concat_axis=0, tiled=True,...  3.61 us
    pallas_call x1, Pallas kernels, body(): pl.pallas_call(lambda *refs: pack_kernel(pairs, capacity, tiles_here, *re...  3.4 us
    ppermute x1, starting transfers between devices, body(): grid_sum = own + lax.ppermute(other, 'tile', swap).astype(jnp.float32)  2.11 us
    pallas_call x1, Pallas kernels, body(): pl.pallas_call(finish_kernel, out_shape=(jax.ShapeDtypeStruct((blocks, 2,...  1.54 us
  transfers between devices with their start and end apart: 3, of which 2 were waited for; matrix products, arithmetic and copies ran while one was open for 0% of the time, Pallas kernels for 0%

profile of v3, /device:TPU:0, one launch (start us, length us, event | category | flops | bytes accessed | tf_op | source)
XLA Modules:
  0.0 47.3 jit_solution(1013610401251079507)
XLA Ops:
  0.6 0.0 copy-start
  0.6 3.4 %pack_blocks.1 = (s32[1216,128]{1,0:T(8,128)}, s32[128]{0:T(128)}) custom-call(s32[128]{0:T(128)} %bitcast.26, s32[128]{0:T(128)} %bitcast.27, f32[256,128]{1,0:T(8,128)} %bitcast.22, s32[256,128]{1,0:T(8,128)} %bitcast.23, s32[256,128]{1,0:T(8,128)} %bitcast.24), custom_call_target="tpu_custom_call" | custom-call | tf_op jit(solution)/shard_map/pack_blocks/pallas_call | solution.py:319
  4.0 5.3 %all-to-all-start = ((s32[8,152,128]{2,1,0:T(8,128)}), s32[8,152,128]{2,1,0:T(8,128)S(1)}, u32[]{:S(2)}, u32[]{:S(2)}) async-start(s32[8,152,128]{2,1,0:T(8,128)} %bitcast.21), calls=%async_computation | async-start | bytes 1245184 | tf_op jit(solution)/shard_map/all_to_all | solution.py:345
  9.3 0.0 copy-start.2
  9.3 0.0 copy-start.1
  9.3 0.7 %copy-done.2 = bf16[16,8,8]{0,2,1:T(8,128)(2,1)S(1)} copy-done((bf16[16,8,8]{0,2,1:T(8,128)(2,1)S(1)}, bf16[16,8,8]{0,2,1:T(8,128)(2,1)}, u32[]{:S(2)}) %copy-start.2) | copy-done | bytes 2072
  10.1 0.1 copy.14.refs_2_
  10.1 0.1 copy-done.1
  10.2 9.7 %all-gather = bf16[1,4,128,256]{3,2,0,1:T(8,128)(2,1)S(1)} all-gather(bf16[1,2,128,256]{3,2,0,1:T(8,128)(2,1)S(1)} %bitcast.25), channel_id=2, replica_groups={{0,16},{2,18},{4,20},{6,22},{8,24},{10,26},{12,28},{14,30},{1,17},{3,19..., dimensions={1}, use_global_device_ids=true | all-gather | bytes 393216 | tf_op jit(solution)/shard_map/all_gather | solution.py:312
  19.9 0.0 copy-done
  20.0 0.0 copy-start.3
  20.0 0.6 %copy-done.3 = s32[128]{0:T(128)S(1)} copy-done((s32[128]{0:T(128)S(1)}, s32[128]{0:T(128)}, u32[]{:S(2)}) %copy-start.3) | copy-done | bytes 536
  20.6 1.4 %all-to-all-done = s32[8,152,128]{2,1,0:T(8,128)S(1)} async-done(((s32[8,152,128]{2,1,0:T(8,128)}), s32[8,152,128]{2,1,0:T(8,128)S(1)}, u32[]{:S(2)}, u32[]{:S(2)}) %all-to-all-start) | async-done | bytes 622624 | tf_op jit(solution)/shard_map/all_to_all | solution.py:345
  22.0 11.3 %grid_blocks.1 = (bf16[392,2,128]{2,1,0:T(2,128)(2,1)}, f32[2,256,128]{2,1,0:T(8,128)S(1)}, bf16[2,256,128]{2,1,0:T(8,128)(2,1)S(1)}) custom-call(s32[1]{0:T(128)} %bitcast.8.refs_0_, s32[1216,128]{1,0:T(8,128)S(1)} %bitcast.18, f32[24,128]{1,0:T(8,128)S(1)} %copy.14.refs_2_, bf16[4,128,256]{2,1,0:T(8,128)(2,1)S(1)} %bitcast.19), custom_call_target="tpu_custom_call" | custom-call | tf_op jit(solution)/shard_map/grid_blocks/pallas_call | solution.py:355
  33.4 2.1 %collective-permute-start = (bf16[2,256,128]{2,1,0:T(8,128)(2,1)S(1)}, bf16[2,256,128]{2,1,0:T(8,128)(2,1)S(1)}, u32[]{:S(2)}, u32[]{:S(2)}) collective-permute-start(bf16[2,256,128]{2,1,0:T(8,128)(2,1)S(1)} %get-tuple-element.19), channel_id=1, source_target_pairs={{0,16},{2,18},{4,20},{6,22},{8,24},{10,26},{12,28},{14,30},{16,0},... | collective-permute-start | bytes 393224 | tf_op jit(solution)/shard_map/ppermute | solution.py:383
  35.5 3.6 %all-to-all-start.1 = ((bf16[392,2,128]{2,1,0:T(2,128)(2,1)}), bf16[392,2,128]{2,1,0:T(2,128)(2,1)S(1)}, u32[]{:S(2)}, u32[]{:S(2)}) async-start(bf16[392,2,128]{2,1,0:T(2,128)(2,1)} %get-tuple-element.17), calls=%async_computation.1 | async-start | bytes 401408 | tf_op jit(solution)/shard_map/all_to_all | solution.py:380
  39.1 0.3 collective-permute-done
  39.4 6.3 %all-gather.1 = bf16[4,256,128]{2,1,0:T(8,128)(2,1)S(1)} all-gather(bf16[2,256,128]{2,1,0:T(8,128)(2,1)S(1)} %add_convert_fusion), channel_id=3, replica_groups=mesh['tile'=16,'freq'=2] {'freq'}, dimensions={0}, use_global_device_ids=true | all-gather | bytes 393216 | tf_op jit(solution)/shard_map/all_gather | solution.py:384
  45.7 0.0 all-to-all-done.1.returned_ref
  45.7 1.5 %finish.1 = (f32[128,2,128]{2,1,0:T(2,128)}, f32[2,128,256]{2,1,0:T(8,128)}) custom-call(f32[2]{0:T(128)S(1)} %dynamic-slice_bitcast_fusion.row_ref, s32[128]{0:T(128)S(1)} %broadcast_add_fusion.slot_ref, bf16[392,2,128]{2,1,0:T(2,128)(2,1)S(1)} %all-to-all-done.1.returned_ref, bf16[2,2,256,128]{3,2,1,0:T(8,128)(2,1)S(1)} %bitcast.20), custom_call_target="tpu_custom_call" | custom-call | tf_op jit(solution)/shard_map/finish/pallas_call | solution.py:385
  (5 shorter events, 0.1 us)
Async XLA Ops:
  0.6 19.3 %copy-start = (f32[2,2]{1,0:T(2,128)S(1)}, f32[2,2]{1,0:T(2,128)}, u32[]{:S(2)}) copy-start(f32[2,2]{1,0:T(2,128)} %param.15) | copy-start | bytes 52
  4.0 18.0 %all-to-all-start = ((s32[8,152,128]{2,1,0:T(8,128)}), s32[8,152,128]{2,1,0:T(8,128)S(1)}, u32[]{:S(2)}, u32[]{:S(2)}) async-start(s32[8,152,128]{2,1,0:T(8,128)} %bitcast.21), calls=%async_computation | async-start | bytes 1245184 | tf_op jit(solution)/shard_map/all_to_all | solution.py:345
  9.3 0.7 %copy-start.2 = (bf16[16,8,8]{0,2,1:T(8,128)(2,1)S(1)}, bf16[16,8,8]{0,2,1:T(8,128)(2,1)}, u32[]{:S(2)}) copy-start(bf16[16,8,8]{0,2,1:T(8,128)(2,1)} %param.14) | copy-start | bytes 6148
  9.3 0.9 %copy-start.1 = (bf16[1,2,128,256]{3,2,1,0:T(8,128)(2,1)S(1)}, bf16[1,2,128,256]{3,2,1,0:T(8,128)(2,1)}, u32[]{:S(2)}) copy-start(bf16[1,2,128,256]{3,2,1,0:T(8,128)(2,1)} %param.13) | copy-start | bytes 393220
  20.0 0.7 %copy-start.3 = (s32[128]{0:T(128)S(1)}, s32[128]{0:T(128)}, u32[]{:S(2)}) copy-start(s32[128]{0:T(128)} %get-tuple-element.12) | copy-start | bytes 1540
  33.4 6.0 %collective-permute-start = (bf16[2,256,128]{2,1,0:T(8,128)(2,1)S(1)}, bf16[2,256,128]{2,1,0:T(8,128)(2,1)S(1)}, u32[]{:S(2)}, u32[]{:S(2)}) collective-permute-start(bf16[2,256,128]{2,1,0:T(8,128)(2,1)S(1)} %get-tuple-element.19), channel_id=1, source_target_pairs={{0,16},{2,18},{4,20},{6,22},{8,24},{10,26},{12,28},{14,30},{16,0},... | collective-permute-start | bytes 393224 | tf_op jit(solution)/shard_map/ppermute | solution.py:383
  35.5 10.2 %all-to-all-start.1 = ((bf16[392,2,128]{2,1,0:T(2,128)(2,1)}), bf16[392,2,128]{2,1,0:T(2,128)(2,1)S(1)}, u32[]{:S(2)}, u32[]{:S(2)}) async-start(bf16[392,2,128]{2,1,0:T(2,128)(2,1)} %get-tuple-element.17), calls=%async_computation.1 | async-start | bytes 401408 | tf_op jit(solution)/shard_map/all_to_all | solution.py:380
